TPU v7x, 256 devices: a whole 4x4x8 slice. The times are simulated.
256 devices in a mesh: freq: 4 (over z_lo), plane: 64 (over y, z_hi, x, core).
Axes of the slice: x: 4, y: 4, z: 8 (z_hi: 2, z_lo: 4; z = z_hi * 4 + z_lo), core: 2. Of those that a mesh axis runs over, the one named last changes fastest.
Arguments:
- wavefield: float32 [4, 2, 2048, 2048], P('freq', None, 'plane'), may hold values from -6 to 6
- inv_table: float32 [4, 8, 2, 128, 128], P('freq'), may hold values from -1 to 1, as said below
- couple_table: float32 [4, 2, 128, 128], P('freq'), may hold values from -1 to 1
- rhs_table: float32 [4, 8, 2], P('freq'), may hold values from -0.25 to 0.25
- recv_index: int32 [2, 16], replicated, may hold values from 0 to 7
- shot_index: int32 [2, 16], replicated, may hold values from 0 to 7
Outputs:
- migrated: float32 [4, 2, 2048, 2048], P('freq', None, 'plane')
- image: float32 [2, 2048], P(None, 'plane')
Inputs may be any that keep to these rules, and one draw needn't show every extreme that they name: `inv_table`: real and imaginary parts of the group inverses.
All inputs are finite; a program needn't handle non-finite values.
Results may differ from a plain program's by a relative error of at most 0.0003.
Values sent between devices are 32-bit elements; how exact they have to be, the bound alone decides.
A program may use at most 64 MiB of HBM per device.

v0:
```python
import functools

import jax
import jax.numpy as jnp
from jax import lax
from jax.experimental import pallas as pl
from jax.experimental.pallas import tpu as pltpu
from jax.sharding import PartitionSpec as P

NX = 2048
GROUP = 128
DEPTHS = 2
NV = 8
GROUPS = NX // GROUP
PLANE = 64
FREQ = 4
LINES = NX // PLANE
HALF = LINES // 2
UNROLL = 4
MESH = pl.DeviceIdType.MESH
F32 = jnp.float32
BF16 = jnp.bfloat16


def split(values):
    high = values.astype(BF16)
    low = (values - high.astype(F32)).astype(BF16)
    return high, low


def dot_nt(left, right):
    return lax.dot_general(left, right, (((1,), (1,)), ((), ())), preferred_element_type=F32)


def dot_nn(left, right):
    return lax.dot_general(left, right, (((1,), (0,)), ((), ())), preferred_element_type=F32)


def product(dot, values, mat_high, mat_low):
    count = values.shape[0]
    high, low = split(values)
    both = dot(jnp.concatenate([high, low], axis=0), mat_high)
    return both[:count] + both[count:] + dot(high, mat_low)


def store_complex(high_ref, low_ref, at, real, imag):
    re_high, re_low = split(real)
    im_high, im_low = split(imag)
    for ref, re_part, im_part in ((high_ref, re_high, im_high), (low_ref, re_low, im_low)):
        ref[at, :GROUP, :GROUP] = re_part
        ref[at, :GROUP, GROUP:] = -im_part
        ref[at, GROUP:, :GROUP] = im_part
        ref[at, GROUP:, GROUP:] = re_part


def swap_blocks(tiles):
    shape = tiles[0].shape
    axis = len(shape) - 1
    lane = lax.broadcasted_iota(jnp.int32, shape, axis)
    lower = lane < 64
    even = (lane // 32) % 2 == 0
    first = [None] * 4
    for a in (0, 1):
        first[a] = jnp.where(lower, tiles[a], pltpu.roll(tiles[a + 2], 64, axis))
        first[a + 2] = jnp.where(lower, pltpu.roll(tiles[a], 64, axis), tiles[a + 2])
    out = [None] * 4
    for a in (0, 2):
        out[a] = jnp.where(even, first[a], pltpu.roll(first[a + 1], 32, axis))
        out[a + 1] = jnp.where(even, pltpu.roll(first[a], 96, axis), first[a + 1])
    return out


def line_pass(src, dst, lines, index, step, inv_high, inv_low, pow_high, pow_low, rhs):
    lane = lax.broadcasted_iota(jnp.int32, (lines, GROUP), 1)
    first = lane == 0
    last = lane == GROUP - 1

    def second_difference(k, part):
        cols = slice(part * GROUP, (part + 1) * GROUP)
        here = src[k + 1, :, cols]
        left = pltpu.roll(jnp.where(last, src[k, :, cols], here), 1, 1)
        right = pltpu.roll(jnp.where(first, src[k + 2, :, cols], here), GROUP - 1, 1)
        return here, left + right - 2.0 * here

    @pl.loop(0, GROUPS // UNROLL)
    def _(outer):
        for inner in range(UNROLL):
            k = outer * UNROLL + inner
            level = index[step, k]
            coef_re = rhs[0, level, 0]
            coef_im = rhs[0, level, 1]
            base_re, second_re = second_difference(k, 0)
            base_im, second_im = second_difference(k, 1)
            source_re = base_re + coef_re * second_re - coef_im * second_im
            source_im = base_im + coef_re * second_im + coef_im * second_re
            source = jnp.concatenate([source_re, source_im], axis=1)
            dst[k + 1] = product(dot_nt, source, inv_high[level], inv_low[level])

    for at, reach in enumerate((1, 2, 4, 8)):
        count = GROUPS - reach
        moved = dst[1 + reach : 1 + GROUPS].reshape(count * lines, 2 * GROUP)
        added = product(dot_nt, moved, pow_high[at], pow_low[at])
        dst[1 : 1 + count] = dst[1 : 1 + count] + added.reshape(count, lines, 2 * GROUP)


def kernel(
    wave_hbm, inv_hbm, couple_hbm, rhs, recv_index, shot_index,
    out, image,
    wave, inv, couple, inv_high, inv_low, pow_high, pow_low,
    field_a, field_b, unit, column_a, column_b,
    fsend, frecv, bsend, brecv,
    vsend, vrecv, wsend, wrecv, isend, irecv,
    in_sem, fwd_send, fwd_recv, back_send, back_recv, img_send, img_recv,
):
    me = lax.axis_index("plane")
    fr = lax.axis_index("freq")
    cross = me % 8
    along = me // 8

    copies = [
        pltpu.make_async_copy(couple_hbm.at[0], couple, in_sem.at[0]),
        pltpu.make_async_copy(inv_hbm.at[0], inv, in_sem.at[1]),
        pltpu.make_async_copy(wave_hbm.at[0], wave, in_sem.at[2]),
    ]
    for copy in copies:
        copy.start()

    def partner(step):
        return (me + step * 9) % PLANE

    barrier = pltpu.get_barrier_semaphore()

    @pl.loop(1, PLANE)
    def _(step):
        pl.semaphore_signal(barrier, inc=1, device_id=(fr, partner(step)), device_id_type=MESH)

    @pl.loop(1, FREQ)
    def _(step):
        pl.semaphore_signal(barrier, inc=1, device_id=((fr + step) % FREQ, me), device_id_type=MESH)

    passes = dict(inv_high=inv_high, inv_low=inv_low, pow_high=pow_high, pow_low=pow_low, rhs=rhs)

    for ref in (field_a, field_b, unit, column_a, column_b):
        pad = jnp.zeros(ref.shape[1:], F32)
        ref[0] = pad
        ref[GROUPS + 1] = pad

    copies[0].wait()
    power_re = couple[0]
    power_im = couple[1]
    for at in range(4):
        store_complex(pow_high, pow_low, at, power_re, power_im)
        if at < 3:
            column = jnp.concatenate([power_re, power_im], axis=0)
            col_high, col_low = split(column)
            high = pow_high[at]
            low = pow_low[at]
            square = dot_nn(high, col_high) + dot_nn(low, col_high) + dot_nn(high, col_low)
            power_re = square[:GROUP]
            power_im = square[GROUP:]
    copies[1].wait()

    @pl.loop(0, NV)
    def _(level):
        store_complex(inv_high, inv_low, level, inv[level, 0], inv[level, 1])

    copies[2].wait()
    for k in range(GROUPS):
        for part in range(2):
            field_a[k + 1, :, part * GROUP : (part + 1) * GROUP] = wave[part, :, k * GROUP : (k + 1) * GROUP]

    line_pass(field_a, field_b, LINES, recv_index, 0, **passes)
    line_pass(field_b, field_a, LINES, recv_index, 1, **passes)

    for big in range(4):
        turned = [
            field_a[1 + 4 * big : 5 + 4 * big, :, part * GROUP : (part + 1) * GROUP]
            .reshape(GROUP, GROUP).T.reshape(4, 4, 8, GROUP)
            for part in range(2)
        ]
        for h in range(2):
            tiles = [turned[part][:, 2 * h + b] for part in range(2) for b in range(2)]
            for y, tile in enumerate(swap_blocks(tiles)):
                first = 4 * (4 * big + y)
                fsend[h, first : first + 4] = tile

    pl.semaphore_wait(barrier, PLANE - 1 + FREQ - 1)

    def exchange(src, dst, h, send, recv):
        @pl.loop(1, PLANE)
        def _(step):
            to = partner(step)
            pltpu.make_async_remote_copy(
                src_ref=src.at[h, to],
                dst_ref=dst.at[h, me],
                send_sem=send.at[h],
                recv_sem=recv.at[h],
                device_id=(fr, to),
                device_id_type=MESH,
            ).start()

        dst[h, me] = src[h, me]

    def all_bytes(ref, h, sem):
        pltpu.make_async_copy(ref.at[h, pl.ds(0, PLANE - 1)], ref.at[h, pl.ds(0, PLANE - 1)], sem.at[h]).wait()

    for h in range(2):
        exchange(fsend, frecv, h, fwd_send, fwd_recv)

    spot = lax.broadcasted_iota(jnp.int32, (LINES, GROUP), 1) - lax.broadcasted_iota(
        jnp.int32, (LINES, GROUP), 0
    )
    for k in range(GROUPS):
        unit[k + 1, :, :GROUP] = (spot == LINES * me - k * GROUP).astype(F32)
        unit[k + 1, :, GROUP:] = jnp.zeros((LINES, GROUP), F32)
    line_pass(unit, field_a, LINES, shot_index, 0, **passes)
    for k in range(GROUPS):
        both = field_a[k + 1] * field_b[k + 1]
        terms = both[:, :GROUP] - both[:, GROUP:]
        vsend[k % 2, k // 2 : k // 2 + 1] = jnp.sum(terms, axis=0, keepdims=True)

    @pl.loop(1, 8)
    def _(step):
        to = (cross + step) % 8
        pltpu.make_async_remote_copy(
            src_ref=vsend.at[to // 4],
            dst_ref=vrecv.at[cross],
            send_sem=img_send.at[0],
            recv_sem=img_recv.at[0],
            device_id=(fr, along * 8 + to),
            device_id_type=MESH,
        ).start()

    vrecv[cross] = vsend[cross // 4]

    lane_row = lax.broadcasted_iota(jnp.int32, (1, GROUP), 1)
    mine = lane_row // LINES == me % 4
    diagonal = jnp.zeros((1, GROUP), F32)
    for h in range(2):
        all_bytes(frecv, h, fwd_recv)
        arrived = frecv[h].reshape(GROUPS, 4, 8, GROUP)
        tiles = swap_blocks([arrived[:, q] for q in range(4)])
        for part in range(2):
            for b in range(2):
                column_a[1 : 1 + GROUPS, b * 8 : b * 8 + 8, part * GROUP : (part + 1) * GROUP] = tiles[2 * part + b]
        line_pass(column_a, column_b, HALF, shot_index, 0, **passes)
        line_pass(column_b, column_a, HALF, shot_index, 1, **passes)
        tiles = [
            column_a[1 : 1 + GROUPS, b * 8 : b * 8 + 8, part * GROUP : (part + 1) * GROUP]
            for part in range(2)
            for b in range(2)
        ]
        bsend[h] = jnp.stack(swap_blocks(tiles), axis=1).reshape(PLANE, 8, GROUP)
        exchange(bsend, brecv, h, back_send, back_recv)
        block = column_a[me // 4 + 1, :, :GROUP]
        row = lax.broadcasted_iota(jnp.int32, (HALF, GROUP), 0)
        lane = lax.broadcasted_iota(jnp.int32, (HALF, GROUP), 1)
        kept = jnp.where(lane == (me % 4) * LINES + h * HALF + row, block, 0.0)
        diagonal = diagonal + jnp.sum(kept, axis=0, keepdims=True)
        if h == 0:
            pltpu.make_async_copy(vrecv.at[pl.ds(0, 7)], vrecv.at[pl.ds(0, 7)], img_recv.at[0]).wait()
            sums = jnp.sum(vrecv[...], axis=0)
            for j in range(8):
                wsend[j] = sums[j : j + 1]

            @pl.loop(1, 8)
            def _(step):
                to = (along + step) % 8
                pltpu.make_async_remote_copy(
                    src_ref=wsend.at[to],
                    dst_ref=wrecv.at[along],
                    send_sem=img_send.at[1],
                    recv_sem=img_recv.at[1],
                    device_id=(fr, to * 8 + cross),
                    device_id_type=MESH,
                ).start()

            wrecv[along] = wsend[along]

    pltpu.make_async_copy(wrecv.at[pl.ds(0, 7)], wrecv.at[pl.ds(0, 7)], img_recv.at[1]).wait()
    summed = jnp.where(mine, jnp.sum(wrecv[...], axis=0), 0.0)

    def folded(values):
        values = values + pltpu.roll(values, 64, 1)
        return values + pltpu.roll(values, 32, 1)

    isend[...] = jnp.zeros((8, GROUP), F32)
    isend[0:1] = folded(summed)
    isend[1:2] = folded(diagonal)

    @pl.loop(1, FREQ)
    def _(step):
        pltpu.make_async_remote_copy(
            src_ref=isend,
            dst_ref=irecv.at[fr],
            send_sem=img_send.at[2],
            recv_sem=img_recv.at[2],
            device_id=((fr + step) % FREQ, me),
            device_id_type=MESH,
        ).start()

    irecv[fr] = isend[...]

    for h in range(2):
        all_bytes(brecv, h, back_recv)
    for big in range(4):
        turned = [[None] * 4, [None] * 4]
        for h in range(2):
            tiles = swap_blocks([brecv[h, 4 * (4 * big + y) : 4 * (4 * big + y) + 4] for y in range(4)])
            for part in range(2):
                for b in range(2):
                    turned[part][2 * h + b] = tiles[2 * part + b]
        for part in range(2):
            block = jnp.stack(turned[part], axis=1).reshape(GROUP, GROUP).T
            for y in range(4):
                at = (4 * big + y) * GROUP
                out[0, part, :, at : at + GROUP] = block[y * LINES : (y + 1) * LINES]

    pltpu.make_async_copy(irecv.at[pl.ds(0, 3)], irecv.at[pl.ds(0, 3)], img_recv.at[2]).wait()
    image[...] = (irecv[0] + irecv[1] + irecv[2] + irecv[3])[:2, :LINES]

    for h in range(2):
        all_bytes(fsend, h, fwd_send)
        all_bytes(bsend, h, back_send)
    pltpu.make_async_copy(vrecv.at[pl.ds(0, 7)], vrecv.at[pl.ds(0, 7)], img_send.at[0]).wait()
    pltpu.make_async_copy(wrecv.at[pl.ds(0, 7)], wrecv.at[pl.ds(0, 7)], img_send.at[1]).wait()
    pltpu.make_async_copy(irecv.at[pl.ds(0, 3)], irecv.at[pl.ds(0, 3)], img_send.at[2]).wait()


def shards(wavefield, inv_table, couple_table, rhs_table, recv_index, shot_index):
    hbm = pl.BlockSpec(memory_space=pl.ANY)
    vmem = pl.BlockSpec(memory_space=pltpu.VMEM)
    smem = pl.BlockSpec(memory_space=pltpu.SMEM)
    tiles = (2, PLANE, 8, GROUP)
    wide = 2 * GROUP
    return pl.pallas_call(
        kernel,
        out_shape=(
            jax.ShapeDtypeStruct((1, 2, LINES, NX), F32),
            jax.ShapeDtypeStruct((DEPTHS, LINES), F32),
        ),
        in_specs=[hbm, hbm, hbm, smem, smem, smem],
        out_specs=(vmem, vmem),
        scratch_shapes=[
            pltpu.VMEM((2, LINES, NX), F32),
            pltpu.VMEM((NV, 2, GROUP, GROUP), F32),
            pltpu.VMEM((2, GROUP, GROUP), F32),
            pltpu.VMEM((NV, wide, wide), BF16),
            pltpu.VMEM((NV, wide, wide), BF16),
            pltpu.VMEM((4, wide, wide), BF16),
            pltpu.VMEM((4, wide, wide), BF16),
            pltpu.VMEM((GROUPS + 2, LINES, wide), F32),
            pltpu.VMEM((GROUPS + 2, LINES, wide), F32),
            pltpu.VMEM((GROUPS + 2, LINES, wide), F32),
            pltpu.VMEM((GROUPS + 2, HALF, wide), F32),
            pltpu.VMEM((GROUPS + 2, HALF, wide), F32),
            pltpu.VMEM(tiles, F32),
            pltpu.VMEM(tiles, F32),
            pltpu.VMEM(tiles, F32),
            pltpu.VMEM(tiles, F32),
            pltpu.VMEM((2, 8, GROUP), F32),
            pltpu.VMEM((8, 8, GROUP), F32),
            pltpu.VMEM((8, 1, GROUP), F32),
            pltpu.VMEM((8, 1, GROUP), F32),
            pltpu.VMEM((8, GROUP), F32),
            pltpu.VMEM((FREQ, 8, GROUP), F32),
            pltpu.SemaphoreType.DMA((3,)),
            pltpu.SemaphoreType.DMA((2,)),
            pltpu.SemaphoreType.DMA((2,)),
            pltpu.SemaphoreType.DMA((2,)),
            pltpu.SemaphoreType.DMA((2,)),
            pltpu.SemaphoreType.DMA((3,)),
            pltpu.SemaphoreType.DMA((3,)),
        ],
        compiler_params=pltpu.CompilerParams(
            collective_id=0, has_side_effects=True, vmem_limit_bytes=40 << 20
        ),
        cost_estimate=pl.CostEstimate(
            flops=5_000_000_000, bytes_accessed=3_000_000, transcendentals=0
        ),
    )(wavefield, inv_table, couple_table, rhs_table, recv_index, shot_index)


def solution(mesh):
    placed = (
        P("freq", None, "plane", None),
        P("freq", None, None, None, None),
        P("freq", None, None, None),
        P("freq", None, None),
        P(),
        P(),
    )
    return jax.shard_map(
        shards,
        mesh=mesh,
        in_specs=placed,
        out_specs=(P("freq", None, "plane", None), P(None, "plane")),
        check_vma=False,
    )
```

profile of v0, /device:TPU:33, one launch (start us, length us, event | category | flops | bytes accessed | tf_op | source)
XLA Modules:
  0.0 58.1 jit_solution(3968487601303165479)
XLA Ops:
  0.6 0.0 copy-start.4
  0.6 0.0 copy-start.3
  0.7 0.8 %copy.8.rhs = f32[1,8,2]{2,1,0:T(8,128)S(1)} copy(f32[1,8,2]{1,2,0:T(2,128)} %param.9) | data formatting | bytes 128 | tf_op args[3]
  1.4 0.0 copy-done.4
  1.4 0.0 copy-done.3
  1.4 0.0 copy-start
  1.4 1.2 %copy-done = f32[1,8,2,128,128]{4,3,2,1,0:T(8,128)S(1)} copy-done((f32[1,8,2,128,128]{4,3,2,1,0:T(8,128)S(1)}, f32[1,8,2,128,128]{4,3,2,1,0:T(8,128)}, u32[]{:S(2)}) %copy-start) | copy-done | bytes 1048600
  2.6 0.0 copy-start.1
  2.6 1.0 %copy-done.1 = f32[1,2,32,2048]{3,2,1,0:T(8,128)S(1)} copy-done((f32[1,2,32,2048]{3,2,1,0:T(8,128)S(1)}, f32[1,2,32,2048]{3,2,1,0:T(8,128)}, u32[]{:S(2)}) %copy-start.1) | copy-done | bytes 524312
  3.7 0.0 copy-start.2
  3.7 0.9 %copy-done.2 = f32[1,2,128,128]{3,2,1,0:T(8,128)S(1)} copy-done((f32[1,2,128,128]{3,2,1,0:T(8,128)S(1)}, f32[1,2,128,128]{3,2,1,0:T(8,128)}, u32[]{:S(2)}) %copy-start.2) | copy-done | bytes 131096
  4.6 52.1 %shard_map.77 = (f32[1,2,32,2048]{3,2,1,0:T(8,128)S(1)}, f32[2,32]{1,0:T(2,128)S(1)}) custom-call(f32[1,2,32,2048]{3,2,1,0:T(8,128)S(1)} %copy-done.1, f32[1,8,2,128,128]{4,3,2,1,0:T(8,128)S(1)} %copy-done, f32[1,2,128,128]{3,2,1,0:T(8,128)S(1)} %copy-done.2, f32[1,8,2]{2,1,0:T(8,128)S(1)} %copy.8.rhs, s32[2,16]{1,0:T(2,128)S(1)} %copy-done.3, ...), custom_call_target="tpu_custom_call" | custom-call | flops 5000000000 | bytes 3000000 | tf_op jit(solution)/shard_map/pallas_call | solution.py:336
  56.7 0.8 %copy.11 = f32[1,2,32,2048]{3,2,1,0:T(8,128)} copy(f32[1,2,32,2048]{3,2,1,0:T(8,128)S(1)} %get-tuple-element.4) | data formatting | bytes 1048576
  57.5 0.6 copy.12
Async XLA Ops:
  0.6 0.8 %copy-start.4 = (s32[2,16]{1,0:T(2,128)S(1)}, s32[2,16]{1,0:T(2,128)}, u32[]{:S(2)}) copy-start(s32[2,16]{1,0:T(2,128)} %shot_index.1) | copy-start | bytes 388
  0.6 0.8 %copy-start.3 = (s32[2,16]{1,0:T(2,128)S(1)}, s32[2,16]{1,0:T(2,128)}, u32[]{:S(2)}) copy-start(s32[2,16]{1,0:T(2,128)} %recv_index.1) | copy-start | bytes 388
  1.4 1.2 %copy-start = (f32[1,8,2,128,128]{4,3,2,1,0:T(8,128)S(1)}, f32[1,8,2,128,128]{4,3,2,1,0:T(8,128)}, u32[]{:S(2)}) copy-start(f32[1,8,2,128,128]{4,3,2,1,0:T(8,128)} %inv_hbm.1) | copy-start | bytes 3145732
  2.6 1.0 %copy-start.1 = (f32[1,2,32,2048]{3,2,1,0:T(8,128)S(1)}, f32[1,2,32,2048]{3,2,1,0:T(8,128)}, u32[]{:S(2)}) copy-start(f32[1,2,32,2048]{3,2,1,0:T(8,128)} %wave_hbm.1) | copy-start | bytes 1572868
  3.7 0.9 %copy-start.2 = (f32[1,2,128,128]{3,2,1,0:T(8,128)S(1)}, f32[1,2,128,128]{3,2,1,0:T(8,128)}, u32[]{:S(2)}) copy-start(f32[1,2,128,128]{3,2,1,0:T(8,128)} %couple_hbm.1) | copy-start | bytes 393220
where the time goes:
time: 58.3 us; the launch traced here: 58.1 us
  Pallas kernels  52.1 us (89%)
  local copies, waits for them, and re-layouts  5.3 us (9%)
  between operations  0.66 us (1%)
    pallas_call x1, Pallas kernels, shards(): pl.pallas_call(kernel, out_shape=(jax.ShapeDtypeStruct((1, 2, LINES, NX),...  52.1 us
    unnamed x13, local copies, waits for them, and re-layouts  5.3 us

commit v1 on v0

--- a/solution.py
+++ b/solution.py
@@ -16,7 +16,6 @@
 FREQ = 4
 LINES = NX // PLANE
 HALF = LINES // 2
-UNROLL = 4
 MESH = pl.DeviceIdType.MESH
 F32 = jnp.float32
 BF16 = jnp.bfloat16
@@ -28,15 +27,11 @@
     return high, low
 
 
-def dot_nt(left, right):
-    return lax.dot_general(left, right, (((1,), (1,)), ((), ())), preferred_element_type=F32)
-
-
-def dot_nn(left, right):
+def dot(left, right):
     return lax.dot_general(left, right, (((1,), (0,)), ((), ())), preferred_element_type=F32)
 
 
-def product(dot, values, mat_high, mat_low):
+def product(values, mat_high, mat_low):
     count = values.shape[0]
     high, low = split(values)
     both = dot(jnp.concatenate([high, low], axis=0), mat_high)
@@ -48,8 +43,8 @@
     im_high, im_low = split(imag)
     for ref, re_part, im_part in ((high_ref, re_high, im_high), (low_ref, re_low, im_low)):
         ref[at, :GROUP, :GROUP] = re_part
-        ref[at, :GROUP, GROUP:] = -im_part
-        ref[at, GROUP:, :GROUP] = im_part
+        ref[at, :GROUP, GROUP:] = im_part
+        ref[at, GROUP:, :GROUP] = -im_part
         ref[at, GROUP:, GROUP:] = re_part
 
 
@@ -82,24 +77,21 @@
         right = pltpu.roll(jnp.where(first, src[k + 2, :, cols], here), GROUP - 1, 1)
         return here, left + right - 2.0 * here
 
-    @pl.loop(0, GROUPS // UNROLL)
-    def _(outer):
-        for inner in range(UNROLL):
-            k = outer * UNROLL + inner
-            level = index[step, k]
-            coef_re = rhs[0, level, 0]
-            coef_im = rhs[0, level, 1]
-            base_re, second_re = second_difference(k, 0)
-            base_im, second_im = second_difference(k, 1)
-            source_re = base_re + coef_re * second_re - coef_im * second_im
-            source_im = base_im + coef_re * second_im + coef_im * second_re
-            source = jnp.concatenate([source_re, source_im], axis=1)
-            dst[k + 1] = product(dot_nt, source, inv_high[level], inv_low[level])
+    for k in range(GROUPS):
+        level = index[step, k]
+        coef_re = rhs[0, 0, level]
+        coef_im = rhs[0, 1, level]
+        base_re, second_re = second_difference(k, 0)
+        base_im, second_im = second_difference(k, 1)
+        source_re = base_re + coef_re * second_re - coef_im * second_im
+        source_im = base_im + coef_re * second_im + coef_im * second_re
+        source = jnp.concatenate([source_re, source_im], axis=1)
+        dst[k + 1] = product(source, inv_high[level], inv_low[level])
 
     for at, reach in enumerate((1, 2, 4, 8)):
         count = GROUPS - reach
         moved = dst[1 + reach : 1 + GROUPS].reshape(count * lines, 2 * GROUP)
-        added = product(dot_nt, moved, pow_high[at], pow_low[at])
+        added = product(moved, pow_high[at], pow_low[at])
         dst[1 : 1 + count] = dst[1 : 1 + count] + added.reshape(count, lines, 2 * GROUP)
 
 
@@ -126,7 +118,7 @@
         copy.start()
 
     def partner(step):
-        return (me + step * 9) % PLANE
+        return (me + step * 33) % PLANE
 
     barrier = pltpu.get_barrier_semaphore()
 
@@ -146,23 +138,20 @@
         ref[GROUPS + 1] = pad
 
     copies[0].wait()
-    power_re = couple[0]
-    power_im = couple[1]
+    power_re = couple[0].T
+    power_im = couple[1].T
     for at in range(4):
         store_complex(pow_high, pow_low, at, power_re, power_im)
         if at < 3:
-            column = jnp.concatenate([power_re, power_im], axis=0)
-            col_high, col_low = split(column)
-            high = pow_high[at]
-            low = pow_low[at]
-            square = dot_nn(high, col_high) + dot_nn(low, col_high) + dot_nn(high, col_low)
-            power_re = square[:GROUP]
-            power_im = square[GROUP:]
+            row = jnp.concatenate([power_re, power_im], axis=1)
+            square = product(row, pow_high[at], pow_low[at])
+            power_re = square[:, :GROUP]
+            power_im = square[:, GROUP:]
     copies[1].wait()
 
     @pl.loop(0, NV)
     def _(level):
-        store_complex(inv_high, inv_low, level, inv[level, 0], inv[level, 1])
+        store_complex(inv_high, inv_low, level, inv[level, 0].T, inv[level, 1].T)
 
     copies[2].wait()
     for k in range(GROUPS):
@@ -328,7 +317,7 @@
 
 
 def shards(wavefield, inv_table, couple_table, rhs_table, recv_index, shot_index):
-    hbm = pl.BlockSpec(memory_space=pl.ANY)
+    hbm = pl.BlockSpec(memory_space=pltpu.HBM)
     vmem = pl.BlockSpec(memory_space=pltpu.VMEM)
     smem = pl.BlockSpec(memory_space=pltpu.SMEM)
     tiles = (2, PLANE, 8, GROUP)
@@ -373,12 +362,12 @@
             pltpu.SemaphoreType.DMA((3,)),
         ],
         compiler_params=pltpu.CompilerParams(
-            collective_id=0, has_side_effects=True, vmem_limit_bytes=40 << 20
+            collective_id=0, has_side_effects=True, vmem_limit_bytes=58 << 20
         ),
         cost_estimate=pl.CostEstimate(
             flops=5_000_000_000, bytes_accessed=3_000_000, transcendentals=0
         ),
-    )(wavefield, inv_table, couple_table, rhs_table, recv_index, shot_index)
+    )(wavefield, inv_table, couple_table, jnp.swapaxes(rhs_table, 1, 2), recv_index, shot_index)
 
 
 def solution(mesh):

time: 58.3 us -> 50.9 us (0.87)
  the two profiles are of different devices: /device:TPU:33 before, /device:TPU:1 now
where the time goes in v1:
time: 50.9 us; the launch traced here: 50.8 us
  Pallas kernels  47.7 us (94%)
  local copies, waits for them, and re-layouts  2.44 us (5%)
  between operations  0.65 us (1%)
    pallas_call x1, Pallas kernels, shards(): pl.pallas_call(kernel, out_shape=(jax.ShapeDtypeStruct((1, 2, LINES, NX),...  47.7 us
    unnamed x4, local copies, waits for them, and re-layouts  2.44 us

profile of v1, /device:TPU:1, one launch (start us, length us, event | category | flops | bytes accessed | tf_op | source)
XLA Modules:
  0.0 50.8 jit_solution(13117065049320228330)
XLA Ops:
  0.6 47.7 %shard_map.77 = (f32[1,2,32,2048]{3,2,1,0:T(8,128)}, f32[2,32]{1,0:T(2,128)}) custom-call(f32[1,2,32,2048]{3,2,1,0:T(8,128)} %wave_hbm.1, f32[1,8,2,128,128]{4,3,2,1,0:T(8,128)} %inv_hbm.1, f32[1,2,128,128]{3,2,1,0:T(8,128)} %couple_hbm.1, f32[1,2,8]{2,1,0:T(2,128)} %bitcast.1, s32[2,16]{1,0:T(2,128)} %recv_index.1, s32[2,16]{1,0:T(2,128)} %shot_index.1), custom_call_target="tpu_custom_call" | custom-call | flops 5000000000 | bytes 3000000 | tf_op jit(solution)/shard_map/pallas_call | solution.py:325
  48.4 0.0 copy-start
  48.4 1.9 %copy.10 = f32[1,2,32,2048]{3,2,1,0:T(8,128)} copy(f32[1,2,32,2048]{3,2,1,0:T(8,128)} %get-tuple-element.4) | data formatting | bytes 1048576
  50.2 0.0 copy-done
  50.2 0.6 %copy.11 = f32[2,32]{1,0:T(2,128)} copy(f32[2,32]{1,0:T(2,128)S(1)} %copy-done) | data formatting | bytes 512
Async XLA Ops:
  48.4 1.9 %copy-start = (f32[2,32]{1,0:T(2,128)S(1)}, f32[2,32]{1,0:T(2,128)}, u32[]{:S(2)}) copy-start(f32[2,32]{1,0:T(2,128)} %get-tuple-element.5) | copy-start | bytes 772

commit v2 on v1

--- a/solution.py
+++ b/solution.py
@@ -161,20 +161,6 @@
     line_pass(field_a, field_b, LINES, recv_index, 0, **passes)
     line_pass(field_b, field_a, LINES, recv_index, 1, **passes)
 
-    for big in range(4):
-        turned = [
-            field_a[1 + 4 * big : 5 + 4 * big, :, part * GROUP : (part + 1) * GROUP]
-            .reshape(GROUP, GROUP).T.reshape(4, 4, 8, GROUP)
-            for part in range(2)
-        ]
-        for h in range(2):
-            tiles = [turned[part][:, 2 * h + b] for part in range(2) for b in range(2)]
-            for y, tile in enumerate(swap_blocks(tiles)):
-                first = 4 * (4 * big + y)
-                fsend[h, first : first + 4] = tile
-
-    pl.semaphore_wait(barrier, PLANE - 1 + FREQ - 1)
-
     def exchange(src, dst, h, send, recv):
         @pl.loop(1, PLANE)
         def _(step):
@@ -194,6 +180,18 @@
         pltpu.make_async_copy(ref.at[h, pl.ds(0, PLANE - 1)], ref.at[h, pl.ds(0, PLANE - 1)], sem.at[h]).wait()
 
     for h in range(2):
+        for big in range(4):
+            turned = [
+                field_a[1 + 4 * big : 5 + 4 * big, :, part * GROUP : (part + 1) * GROUP]
+                .reshape(GROUP, GROUP).T.reshape(4, 4, 8, GROUP)
+                for part in range(2)
+            ]
+            tiles = [turned[part][:, 2 * h + b] for part in range(2) for b in range(2)]
+            for y, tile in enumerate(swap_blocks(tiles)):
+                first = 4 * (4 * big + y)
+                fsend[h, first : first + 4] = tile
+        if h == 0:
+            pl.semaphore_wait(barrier, PLANE - 1 + FREQ - 1)
         exchange(fsend, frecv, h, fwd_send, fwd_recv)
 
     spot = lax.broadcasted_iota(jnp.int32, (LINES, GROUP), 1) - lax.broadcasted_iota(

time: 50.9 us -> 51 us (level)
  no operation moved by 1% of the time
where the time goes in v2:
time: 51 us; the launch traced here: 50.9 us
  Pallas kernels  47.8 us (94%)
  local copies, waits for them, and re-layouts  2.44 us (5%)
  between operations  0.65 us (1%)
    pallas_call x1, Pallas kernels, shards(): pl.pallas_call(kernel, out_shape=(jax.ShapeDtypeStruct((1, 2, LINES, NX),...  47.8 us
    unnamed x4, local copies, waits for them, and re-layouts  2.44 us

profile of v2, /device:TPU:1, one launch (start us, length us, event | category | flops | bytes accessed | tf_op | source)
XLA Modules:
  0.0 50.9 jit_solution(5175260242184440765)
XLA Ops:
  0.6 47.8 %shard_map.77 = (f32[1,2,32,2048]{3,2,1,0:T(8,128)}, f32[2,32]{1,0:T(2,128)}) custom-call(f32[1,2,32,2048]{3,2,1,0:T(8,128)} %wave_hbm.1, f32[1,8,2,128,128]{4,3,2,1,0:T(8,128)} %inv_hbm.1, f32[1,2,128,128]{3,2,1,0:T(8,128)} %couple_hbm.1, f32[1,2,8]{2,1,0:T(2,128)} %bitcast.1, s32[2,16]{1,0:T(2,128)} %recv_index.1, s32[2,16]{1,0:T(2,128)} %shot_index.1), custom_call_target="tpu_custom_call" | custom-call | flops 5000000000 | bytes 3000000 | tf_op jit(solution)/shard_map/pallas_call | solution.py:323
  48.4 0.0 copy-start
  48.4 1.9 %copy.10 = f32[1,2,32,2048]{3,2,1,0:T(8,128)} copy(f32[1,2,32,2048]{3,2,1,0:T(8,128)} %get-tuple-element.4) | data formatting | bytes 1048576
  50.3 0.0 copy-done
  50.3 0.6 %copy.11 = f32[2,32]{1,0:T(2,128)} copy(f32[2,32]{1,0:T(2,128)S(1)} %copy-done) | data formatting | bytes 512
Async XLA Ops:
  48.4 1.9 %copy-start = (f32[2,32]{1,0:T(2,128)S(1)}, f32[2,32]{1,0:T(2,128)}, u32[]{:S(2)}) copy-start(f32[2,32]{1,0:T(2,128)} %get-tuple-element.5) | copy-start | bytes 772

commit v3 on v2

--- a/solution.py
+++ b/solution.py
@@ -288,12 +288,21 @@
 
     irecv[fr] = isend[...]
 
-    for h in range(2):
-        all_bytes(brecv, h, back_recv)
+    def rows_of(h, big):
+        return [brecv[h, 4 * (4 * big + y) : 4 * (4 * big + y) + 4] for y in range(4)]
+
+    all_bytes(brecv, 0, back_recv)
+    for big in range(4):
+        for y, tile in enumerate(swap_blocks(rows_of(0, big))):
+            first = 4 * (4 * big + y)
+            brecv[0, first : first + 4] = tile
+    all_bytes(brecv, 1, back_recv)
     for big in range(4):
         turned = [[None] * 4, [None] * 4]
         for h in range(2):
-            tiles = swap_blocks([brecv[h, 4 * (4 * big + y) : 4 * (4 * big + y) + 4] for y in range(4)])
+            tiles = rows_of(h, big)
+            if h == 1:
+                tiles = swap_blocks(tiles)
             for part in range(2):
                 for b in range(2):
                     turned[part][2 * h + b] = tiles[2 * part + b]

time: 51 us -> 50.7 us (level)
  no operation moved by 1% of the time
where the time goes in v3:
time: 50.7 us; the launch traced here: 50.6 us
  Pallas kernels  47.5 us (94%)
  local copies, waits for them, and re-layouts  2.44 us (5%)
  between operations  0.65 us (1%)
    pallas_call x1, Pallas kernels, shards(): pl.pallas_call(kernel, out_shape=(jax.ShapeDtypeStruct((1, 2, LINES, NX),...  47.5 us
    unnamed x4, local copies, waits for them, and re-layouts  2.44 us

profile of v3, /device:TPU:1, one launch (start us, length us, event | category | flops | bytes accessed | tf_op | source)
XLA Modules:
  0.0 50.6 jit_solution(15219687056020887938)
XLA Ops:
  0.6 47.5 %shard_map.77 = (f32[1,2,32,2048]{3,2,1,0:T(8,128)}, f32[2,32]{1,0:T(2,128)}) custom-call(f32[1,2,32,2048]{3,2,1,0:T(8,128)} %wave_hbm.1, f32[1,8,2,128,128]{4,3,2,1,0:T(8,128)} %inv_hbm.1, f32[1,2,128,128]{3,2,1,0:T(8,128)} %couple_hbm.1, f32[1,2,8]{2,1,0:T(2,128)} %bitcast.1, s32[2,16]{1,0:T(2,128)} %recv_index.1, s32[2,16]{1,0:T(2,128)} %shot_index.1), custom_call_target="tpu_custom_call" | custom-call | flops 5000000000 | bytes 3000000 | tf_op jit(solution)/shard_map/pallas_call | solution.py:332
  48.1 0.0 copy-start
  48.2 1.9 %copy.10 = f32[1,2,32,2048]{3,2,1,0:T(8,128)} copy(f32[1,2,32,2048]{3,2,1,0:T(8,128)} %get-tuple-element.4) | data formatting | bytes 1048576
  50.0 0.0 copy-done
  50.0 0.6 %copy.11 = f32[2,32]{1,0:T(2,128)} copy(f32[2,32]{1,0:T(2,128)S(1)} %copy-done) | data formatting | bytes 512
Async XLA Ops:
  48.1 1.9 %copy-start = (f32[2,32]{1,0:T(2,128)S(1)}, f32[2,32]{1,0:T(2,128)}, u32[]{:S(2)}) copy-start(f32[2,32]{1,0:T(2,128)} %get-tuple-element.5) | copy-start | bytes 772
